TPU v7x, 32 devices: a whole 2x2x4 slice. The times are simulated.
32 devices in a mesh: rep: 8 (over z, core), fsdp: 4 (over y, x).
Axes of the slice: x: 2, y: 2, z: 4, core: 2. Of those that a mesh axis runs over, the one named last changes fastest.
Arguments:
- tokens: bfloat16 [512, 4096], P('fsdp', 'rep'), may hold values from -6 to 6
- grad_out: bfloat16 [512, 4096], P('fsdp', 'rep'), may hold values from -6 to 6
- w_gate: bfloat16 [4096, 24576], P('fsdp', 'rep'), may hold values from -0.125 to 0.125
- w_up: bfloat16 [4096, 24576], P('fsdp', 'rep'), may hold values from -0.125 to 0.125
- w_down: bfloat16 [24576, 4096], P('rep', 'fsdp'), may hold values from -0.0390625 to 0.0390625
Outputs:
- grad_tokens: bfloat16 [512, 4096], P('fsdp', 'rep')
- grad_gate: bfloat16 [4096, 24576], P('fsdp', 'rep')
- grad_up: bfloat16 [4096, 24576], P('fsdp', 'rep')
- grad_down: bfloat16 [24576, 4096], P('rep', 'fsdp')
All inputs are finite; a program needn't handle non-finite values.
Results may differ from a plain program's by a relative error of at most 0.0049.
Values may be sent and summed in bfloat16 or wider, within the bound.
A program may use at most 192 MiB of HBM per device.

v0:
```python
import math

import jax
import jax.numpy as jnp
from jax import lax
from jax.sharding import PartitionSpec as P

HB = 128


def hadamard(size):
    index = jnp.arange(size, dtype=jnp.int32)
    both = index[:, None] & index[None, :]
    parity = jnp.zeros((size, size), jnp.int32)
    for bit_pos in range(size.bit_length() - 1):
        parity = parity + (both >> bit_pos & 1)
    return (1 - 2 * (parity % 2)).astype(jnp.float32) / math.sqrt(size)


def contract_first(left, right):
    return lax.dot_general(
        left, right, (((0,), (0,)), ((), ())), preferred_element_type=jnp.float32
    )


def contract_last(left, right):
    return lax.dot_general(
        left, right, (((1,), (1,)), ((), ())), preferred_element_type=jnp.float32
    )


def body(tokens, grad_out, w_gate, w_up, w_down):
    x_full, dy_full = (
        lax.all_gather(tokens, "rep", axis=1, tiled=True),
        lax.all_gather(grad_out, "rep", axis=1, tiled=True),
    )
    gate_full, up_full = (
        lax.all_gather(w_gate, "fsdp", axis=0, tiled=True),
        lax.all_gather(w_up, "fsdp", axis=0, tiled=True),
    )
    x_block, dy_block = (
        lax.all_to_all(x_full, "fsdp", split_axis=1, concat_axis=0, tiled=True),
        lax.all_to_all(dy_full, "fsdp", split_axis=1, concat_axis=0, tiled=True),
    )
    gate = jnp.dot(x_full, gate_full, preferred_element_type=jnp.float32)
    up = jnp.dot(x_full, up_full, preferred_element_type=jnp.float32)
    d_hidden = contract_last(dy_full, lax.all_gather(w_down, "fsdp", axis=1, tiled=True))
    sig = jax.nn.sigmoid(gate)
    active = gate * sig
    hidden = (active * up).astype(jnp.bfloat16)
    d_gate = (d_hidden * up * sig * (1.0 + gate * (1.0 - sig))).astype(jnp.bfloat16)
    d_up = (d_hidden * active).astype(jnp.bfloat16)
    partial_x = contract_last(d_gate, gate_full) + contract_last(d_up, up_full)
    grad_tokens = lax.psum_scatter(partial_x, "rep", scatter_dimension=1, tiled=True).astype(
        jnp.bfloat16
    )
    width_rows = x_block.shape[1]
    hidden_cols = d_gate.shape[1]
    gw_gate = contract_first(x_block, lax.all_gather(d_gate, "fsdp", axis=0, tiled=True))
    gw_up = contract_first(x_block, lax.all_gather(d_up, "fsdp", axis=0, tiled=True))
    gw_down = contract_first(lax.all_gather(hidden, "fsdp", axis=0, tiled=True), dy_block)
    rotor = hadamard(HB)
    blocks_count = width_rows // HB

    def rotate_rows(grad):
        blocks = grad.reshape(blocks_count, HB, hidden_cols)
        return (
            jnp.einsum("ij,bjf->bif", rotor, blocks, precision=lax.Precision.HIGHEST)
            .reshape(width_rows, hidden_cols)
            .astype(jnp.bfloat16)
        )

    blocks = gw_down.reshape(hidden_cols, blocks_count, HB)
    grad_down = (
        jnp.einsum("fbj,ij->fbi", blocks, rotor, precision=lax.Precision.HIGHEST)
        .reshape(hidden_cols, width_rows)
        .astype(jnp.bfloat16)
    )
    return (grad_tokens, rotate_rows(gw_gate), rotate_rows(gw_up), grad_down)


def solution(mesh):
    return jax.shard_map(
        body,
        mesh=mesh,
        in_specs=(
            P("fsdp", "rep"),
            P("fsdp", "rep"),
            P("fsdp", "rep"),
            P("fsdp", "rep"),
            P("rep", "fsdp"),
        ),
        out_specs=(P("fsdp", "rep"), P("fsdp", "rep"), P("fsdp", "rep"), P("rep", "fsdp")),
        check_vma=False,
    )
```

profile of v0, /device:TPU:2, one launch (start us, length us, event | category | flops | bytes accessed | tf_op | source)
XLA Modules:
  0.0 1007.2 jit_solution(15444378278853370528)
XLA Ops:
  7.2 0.0 copy-start.5
  7.2 0.0 all-gather.9.cloned.1.call-start
  7.2 1.7 copy.11
  8.9 0.0 all-gather.9.cloned.1.call-update
  8.9 0.0 all-gather.11.cloned.1.call-start
  9.0 0.7 all-gather.11.cloned.1.call-update
  9.7 0.0 all-gather.13.cloned.1.call-start
  9.7 0.0 copy-done.5
  9.7 0.8 copy.12
  10.5 0.0 all-gather.13.cloned.1.call-update
  10.5 0.0 all-gather.17.cloned.1.call-start
  10.6 0.5 all-gather.17.cloned.1.call-update
  11.1 0.0 all-gather.15.cloned.1.call-start
  11.2 0.5 all-gather.15.cloned.1.call-update
  11.7 0.0 reduce-scatter.2.cloned.1.call-start
  11.7 21.8 %all-gather.9.cloned.1.call-done = bf16[128,4096]{0,1:T(8,128)(2,1)} async-done(((bf16[128,512]{0,1:T(8,128)(2,1)}), bf16[128,4096]{0,1:T(8,128)(2,1)}) %all-gather.9.cloned.1.call-update) | async-done | bytes 1048592 | tf_op jit(solution)/shard_map/all_gather | solution.py:35
  33.5 229.2 %all-gather.11.cloned.1.call-done = bf16[3072,4096]{1,0:T(8,128)(2,1)} async-done(((bf16[3072,1024]{1,0:T(8,128)(2,1)}), bf16[3072,4096]{1,0:T(8,128)(2,1)}) %all-gather.11.cloned.1.call-update) | async-done | bytes 25165840 | tf_op jit(solution)/shard_map/all_gather | solution.py:47
  262.8 14.1 %fusion.60 = f32[128,3072]{1,0:T(8,128)} fusion(bf16[128,4096]{0,1:T(8,128)(2,1)} %all-gather.9.cloned.1.call-done, bf16[3072,4096]{1,0:T(8,128)(2,1)} %all-gather.11.cloned.1.call-done), kind=kOutput, calls=%fused_computation.68 | convolution fusion | flops 3221225472 | bytes 27787264 | tf_op jit(solution)/shard_map/dot_general | solution.py:27
  276.9 10.2 %all-gather.13.cloned.1.call-done = bf16[128,4096]{0,1:T(8,128)(2,1)} async-done(((bf16[128,512]{0,1:T(8,128)(2,1)}), bf16[128,4096]{0,1:T(8,128)(2,1)}) %all-gather.13.cloned.1.call-update) | async-done | bytes 1048592 | tf_op jit(solution)/shard_map/all_gather | solution.py:34
  287.1 0.0 copy-start.1
  287.1 229.1 %all-gather.17.cloned.1.call-done = bf16[4096,3072]{1,0:T(8,128)(2,1)} async-done(((bf16[1024,3072]{1,0:T(8,128)(2,1)}), bf16[4096,3072]{1,0:T(8,128)(2,1)}) %all-gather.17.cloned.1.call-update) | async-done | bytes 25165840 | tf_op jit(solution)/shard_map/all_gather | solution.py:38
  516.2 13.1 %fusion.61 = f32[128,3072]{1,0:T(8,128)} fusion(bf16[128,4096]{0,1:T(8,128)(2,1)} %all-gather.13.cloned.1.call-done, bf16[4096,3072]{1,0:T(8,128)(2,1)} %all-gather.17.cloned.1.call-done), kind=kOutput, calls=%fused_computation.69 | convolution fusion | flops 3221225472 | bytes 27787264 | tf_op jit(solution)/shard_map/dot_general | solution.py:45
  529.3 216.4 %all-gather.15.cloned.1.call-done = bf16[4096,3072]{1,0:T(8,128)(2,1)} async-done(((bf16[1024,3072]{1,0:T(8,128)(2,1)}), bf16[4096,3072]{1,0:T(8,128)(2,1)}) %all-gather.15.cloned.1.call-update) | async-done | bytes 25165840 | tf_op jit(solution)/shard_map/all_gather | solution.py:39
  745.6 0.0 copy-done.1
  745.6 14.1 %multiply_convert_fusion = (bf16[128,3072]{1,0:T(8,128)(2,1)}, bf16[128,3072]{1,0:T(8,128)(2,1)S(1)}, bf16[128,3072]{1,0:T(8,128)(2,1)S(1)}) fusion(f32[128,3072]{1,0:T(8,128)} %fusion.61, f32[128,3072]{1,0:T(8,128)} %fusion.60, bf16[128,4096]{0,1:T(8,128)(2,1)S(1)} %copy-done.1, bf16[4096,3072]{1,0:T(8,128)(2,1)} %all-gather.15.cloned.1.call-done), kind=kOutput, calls=%fused_computation.6 | convolution fusion | flops 3227123712 | bytes 31719424 | tf_op jit(solution)/shard_map/dot_general | solution.py:46
  759.8 0.0 copy-start.2
  759.8 0.0 copy-start.3
  759.8 24.3 %fusion.62 = f32[128,4096]{1,0:T(8,128)} fusion(bf16[128,3072]{1,0:T(8,128)(2,1)S(1)} %get-tuple-element.17, bf16[4096,3072]{1,0:T(8,128)(2,1)} %all-gather.17.cloned.1.call-done), kind=kOutput, calls=%fused_computation.70 | convolution fusion | flops 3221225472 | bytes 28049408 | tf_op jit(solution)/shard_map/dot_general | solution.py:27
  784.0 0.0 copy-done.2
  784.0 0.0 copy-done.3
  784.0 15.1 %convolution_add_fusion = f32[128,4096]{1,0:T(8,128)} fusion(f32[128,4096]{1,0:T(8,128)} %fusion.62, bf16[128,3072]{1,0:T(8,128)(2,1)S(1)} %get-tuple-element.18, bf16[4096,3072]{1,0:T(8,128)(2,1)} %all-gather.15.cloned.1.call-done), kind=kOutput, calls=%fused_computation.3 | convolution fusion | flops 3221749760 | bytes 30146560 | tf_op jit(solution)/shard_map/dot_general | solution.py:27
  799.1 0.0 reduce-scatter.2.cloned.1.call-update
  799.2 0.0 all-gather.21.cloned.1.call-start
  799.2 0.7 all-gather.21.cloned.1.call-update
  799.9 0.0 all-gather.19.cloned.1.call-start
  800.0 0.7 all-gather.19.cloned.1.call-update
  800.7 0.0 all-gather.23.cloned.1.call-start
  800.7 0.7 all-gather.23.cloned.1.call-update
  801.4 16.3 %all_to_all.38 = bf16[128,4,1024]{0,2,1:T(8,128)(2,1)S(1)} all-to-all(bf16[128,4,1024]{0,2,1:T(8,128)(2,1)S(1)} %bitcast.51), channel_id=1, replica_groups=mesh['rep'=8,'fsdp'=4] {'fsdp'}, dimensions={1} | all-to-all | bytes 2097152 | tf_op jit(solution)/shard_map/all_to_all | solution.py:42
  817.7 4.6 all-to-all-start.1
  822.3 0.5 copy.13
  822.8 0.0 copy-start.4
  822.8 11.5 %all-to-all-done.1 = bf16[128,4,1024]{0,2,1:T(8,128)(2,1)S(1)} async-done(((bf16[128,4,1024]{0,2,1:T(8,128)(2,1)}), bf16[128,4,1024]{0,2,1:T(8,128)(2,1)S(1)}, u32[]{:S(2)}, u32[]{:S(2)}) %all-to-all-start.1) | async-done | bytes 1048608 | tf_op jit(solution)/shard_map/all_to_all | solution.py:43
  834.4 0.5 copy.14
  834.9 1.3 copy.15
  836.2 0.0 reduce-scatter.2.cloned.1.call-done
  836.2 1.6 convert_element_type.45
  837.9 41.8 %all-gather.21.cloned.1.call-done = bf16[512,3072]{1,0:T(8,128)(2,1)} async-done(((bf16[128,3072]{1,0:T(8,128)(2,1)}), bf16[512,3072]{1,0:T(8,128)(2,1)}) %all-gather.21.cloned.1.call-update) | async-done | bytes 3145744 | tf_op jit(solution)/shard_map/all_gather | solution.py:60
  879.6 8.2 fusion.64
  887.9 0.0 copy-done.4
  887.9 38.2 %all-gather.19.cloned.1.call-done = bf16[512,3072]{1,0:T(8,128)(2,1)} async-done(((bf16[128,3072]{1,0:T(8,128)(2,1)}), bf16[512,3072]{1,0:T(8,128)(2,1)}) %all-gather.19.cloned.1.call-update) | async-done | bytes 3145744 | tf_op jit(solution)/shard_map/all_gather | solution.py:59
  926.0 0.0 copy-start
  926.0 5.8 fusion.63
  931.8 0.0 copy-done
  931.9 13.7 %convolution_convert_fusion.1 = bf16[8,3072,128]{1,2,0:T(8,128)(2,1)} fusion(f32[8,128,3072]{2,1,0:T(8,128)S(1)} %bitcast.49), kind=kOutput, calls=%fused_computation.1 | convolution fusion | flops 4835573760 | bytes 18874368 | tf_op jit(solution)/shard_map/ij,bjf->bif/dot_general | solution.py:68
  945.6 13.7 %convolution_convert_fusion.2 = bf16[8,3072,128]{1,2,0:T(8,128)(2,1)} fusion(f32[8,128,3072]{2,1,0:T(8,128)S(1)} %bitcast.50), kind=kOutput, calls=%fused_computation.2 | convolution fusion | flops 4835573760 | bytes 18874368 | tf_op jit(solution)/shard_map/ij,bjf->bif/dot_general | solution.py:68
  959.3 12.6 %all-gather.23.cloned.1.call-done = bf16[512,3072]{1,0:T(8,128)(2,1)} async-done(((bf16[128,3072]{1,0:T(8,128)(2,1)}), bf16[512,3072]{1,0:T(8,128)(2,1)}) %all-gather.23.cloned.1.call-update) | async-done | bytes 3145744 | tf_op jit(solution)/shard_map/all_gather | solution.py:61
  971.9 5.7 fusion
  977.6 14.0 %convolution_convert_fusion = bf16[3072,8,128]{0,2,1:T(8,128)(2,1)} fusion(f32[3072,8,128]{2,0,1:T(8,128)S(1)} %fusion), kind=kOutput, calls=%fused_computation | convolution fusion | flops 4835573760 | bytes 18874368 | tf_op jit(solution)/shard_map/fbj,ij->fbi/dot_general | solution.py:75
  991.6 8.6 copy.17
Async XLA Ops:
  7.2 2.6 copy-start.5
  7.2 26.4 %all-gather.9.cloned.1.call-start = ((), (), s32[]{:S(2)}) async-start(), calls=%async_computation.3 | async-start | bytes 1179648 | tf_op jit(solution)/shard_map/all_gather | solution.py:35
  8.9 253.8 %all-gather.11.cloned.1.call-start = ((), (), s32[]{:S(2)}) async-start(), calls=%async_computation.4 | async-start | bytes 31457280 | tf_op jit(solution)/shard_map/all_gather | solution.py:47
  9.7 277.4 %all-gather.13.cloned.1.call-start = ((), (), s32[]{:S(2)}) async-start(), calls=%async_computation.5 | async-start | bytes 1179648 | tf_op jit(solution)/shard_map/all_gather | solution.py:34
  10.5 505.6 %all-gather.17.cloned.1.call-start = ((), (), s32[]{:S(2)}) async-start(), calls=%async_computation.7 | async-start | bytes 31457280 | tf_op jit(solution)/shard_map/all_gather | solution.py:38
  11.1 734.5 %all-gather.15.cloned.1.call-start = ((), (), s32[]{:S(2)}) async-start(), calls=%async_computation.6 | async-start | bytes 31457280 | tf_op jit(solution)/shard_map/all_gather | solution.py:39
  11.7 824.5 %reduce-scatter.2.cloned.1.call-start = ((), (), s32[]{:S(2)}) async-start(), calls=%async_computation.8 | async-start | bytes 2359296 | tf_op jit(solution)/shard_map/reduce_scatter | solution.py:54
  287.1 458.6 %copy-start.1 = (bf16[128,4096]{0,1:T(8,128)(2,1)S(1)}, bf16[128,4096]{0,1:T(8,128)(2,1)}, u32[]{:S(2)}) copy-start(bf16[128,4096]{0,1:T(8,128)(2,1)} %all-gather.13.cloned.1.call-done) | copy-start | bytes 3145732
  759.8 24.3 %copy-start.2 = (bf16[128,3072]{1,0:T(8,128)(2,1)}, bf16[128,3072]{1,0:T(8,128)(2,1)S(1)}, u32[]{:S(2)}) copy-start(bf16[128,3072]{1,0:T(8,128)(2,1)S(1)} %get-tuple-element.17) | copy-start | bytes 2359300
  759.8 24.3 %copy-start.3 = (bf16[128,3072]{1,0:T(8,128)(2,1)}, bf16[128,3072]{1,0:T(8,128)(2,1)S(1)}, u32[]{:S(2)}) copy-start(bf16[128,3072]{1,0:T(8,128)(2,1)S(1)} %get-tuple-element.18) | copy-start | bytes 2359300
  799.2 80.4 %all-gather.21.cloned.1.call-start = ((), (), s32[]{:S(2)}) async-start(), calls=%async_computation.10 | async-start | bytes 3932160 | tf_op jit(solution)/shard_map/all_gather | solution.py:60
  799.9 126.1 %all-gather.19.cloned.1.call-start = ((), (), s32[]{:S(2)}) async-start(), calls=%async_computation.9 | async-start | bytes 3932160 | tf_op jit(solution)/shard_map/all_gather | solution.py:59
  800.7 171.2 %all-gather.23.cloned.1.call-start = ((), (), s32[]{:S(2)}) async-start(), calls=%async_computation.11 | async-start | bytes 3932160 | tf_op jit(solution)/shard_map/all_gather | solution.py:61
  817.7 16.7 %all-to-all-start.1 = ((bf16[128,4,1024]{0,2,1:T(8,128)(2,1)}), bf16[128,4,1024]{0,2,1:T(8,128)(2,1)S(1)}, u32[]{:S(2)}, u32[]{:S(2)}) async-start(bf16[128,4,1024]{0,2,1:T(8,128)(2,1)} %bitcast.13), calls=%async_computation.2 | async-start | bytes 2097152 | tf_op jit(solution)/shard_map/all_to_all | solution.py:43
  822.8 65.0 %copy-start.4 = (bf16[4,128,1024]{2,1,0:T(8,128)(2,1)}, bf16[4,128,1024]{2,1,0:T(8,128)(2,1)S(1)}, u32[]{:S(2)}) copy-start(bf16[4,128,1024]{2,1,0:T(8,128)(2,1)S(1)} %copy.13) | copy-start | bytes 3145732
  926.0 5.8 copy-start
Sparse Core Ops, SparseCore 0:
  10.2 23.3 all-gather.8
  35.4 227.3 all-gather.10
  265.0 22.0 all-gather.12
  288.8 227.3 all-gather.16
  517.9 227.6 all-gather.14
  799.3 35.6 reduce-scatter.1
  836.9 42.7 all-gather.20
  882.0 43.9 all-gather.18
  927.9 43.9 all-gather.22
where the time goes:
time: 1010 us
  waiting for transfers between devices  815 us (81%)
  matrix products  142 us (14%)
  blocking collectives  16.3 us (2%)
  between operations  14.3 us (1%)
  local copies, waits for them, and re-layouts  13.5 us (1%)
    all_gather x1, waiting for transfers between devices, body(): lax.all_gather(w_down, 'fsdp', axis=1, tiled=True)  229 us
    all_gather x1, waiting for transfers between devices, body(): lax.all_gather(w_gate, 'fsdp', axis=0, tiled=True)  229 us
    all_gather x1, waiting for transfers between devices, body(): lax.all_gather(w_up, 'fsdp', axis=0, tiled=True)  216 us
    dot_general x3, matrix products, contract_last(): lax.dot_general(left, right, (((1,), (1,)), ((), ())), preferred_element_...  53.5 us
    all_gather x1, waiting for transfers between devices, body(): lax.all_gather(d_up, 'fsdp', axis=0, tiled=True)  41.8 us
    all_gather x1, waiting for transfers between devices, body(): lax.all_gather(d_gate, 'fsdp', axis=0, tiled=True)  38.2 us
    dot_general x2, matrix products, rotate_rows(): jnp.einsum('ij,bjf->bif', rotor, blocks, precision=lax.Precision.HIGHEST)  27.4 us
    all_gather x1, waiting for transfers between devices, body(): lax.all_gather(grad_out, 'rep', axis=1, tiled=True)  21.8 us
  transfers between devices with their start and end apart: 10, of which 9 were waited for; matrix products, arithmetic and copies ran while one was open for 7% of the time, Pallas kernels for 0%

commit v1 on v0

v1 whole, which is shorter than its diff:
```python
import functools
import math

import jax
import jax.numpy as jnp
from jax import lax
from jax.experimental import pallas as pl
from jax.experimental.pallas import tpu as pltpu
from jax.sharding import PartitionSpec as P

HB = 128
BF16 = jnp.bfloat16
F32 = jnp.float32


def hadamard(size):
    index = jnp.arange(size, dtype=jnp.int32)
    both = index[:, None] & index[None, :]
    parity = jnp.zeros((size, size), jnp.int32)
    for bit_pos in range(size.bit_length() - 1):
        parity = parity + (both >> bit_pos & 1)
    return (1 - 2 * (parity % 2)).astype(F32) / math.sqrt(size)


def dot_dims(left, right, left_dim, right_dim, kind=F32):
    return lax.dot_general(
        left, right, (((left_dim,), (right_dim,)), ((), ())), preferred_element_type=kind
    )


def rotate_features(block):
    rows, width = block.shape
    parts = block.astype(F32).reshape(rows, width // HB, HB)
    turned = jnp.einsum("tbj,ij->tbi", parts, hadamard(HB), precision=lax.Precision.HIGHEST)
    return turned.reshape(rows, width).astype(BF16)


def gather_blocks(tokens, grad_out):
    both = jnp.stack([tokens, grad_out])
    full = lax.all_gather(both, "rep", axis=2, tiled=True)
    block = lax.all_to_all(full, "fsdp", split_axis=2, concat_axis=1, tiled=True)
    return block[0], block[1]


def activations(gate, up, d_hidden):
    sig = jax.nn.sigmoid(gate)
    active = gate * sig
    hidden = (active * up).astype(BF16)
    d_gate = (d_hidden * up * sig * (1.0 + gate * (1.0 - sig))).astype(BF16)
    d_up = (d_hidden * active).astype(BF16)
    return hidden, d_gate, d_up


def middle_plain(x_block, dy_block, w_gate, w_up, w_down):
    sums = [
        lax.psum_scatter(part, "fsdp", scatter_dimension=0, tiled=True)
        for part in (
            dot_dims(x_block, w_gate, 1, 0),
            dot_dims(x_block, w_up, 1, 0),
            dot_dims(dy_block, w_down, 1, 1),
        )
    ]
    own = activations(*sums)
    hidden, d_gate, d_up = [lax.all_gather(v, "fsdp", axis=0, tiled=True) for v in own]
    partial = dot_dims(d_gate, w_gate, 1, 1) + dot_dims(d_up, w_up, 1, 1)
    return hidden, d_gate, d_up, partial


MESH = pl.DeviceIdType.MESH
LAG = 2


def middle_kernel(
    n, x_ref, dy_ref, wg_hbm, wu_hbm, wd_hbm, hid_out, dg_out, du_out, total,
    w_pair, w_low, part, send1, recv1, send2, recv2, acts,
    w_sem, out_sem, ssem, rsem,
):
    chunk = w_low.shape[1]
    slots = part.shape[0]
    outs = (hid_out, dg_out, du_out)
    me = lax.axis_index("fsdp")
    y, x = me // 2, me % 2
    near_x, near_y = 2 * y + 1 - x, 2 * (1 - y) + x

    def span(c):
        return pl.ds(pl.multiple_of(c * chunk, chunk), chunk)

    def weights(c):
        return (
            pltpu.make_async_copy(wg_hbm.at[:, span(c)], w_pair.at[c, :, pl.ds(0, chunk)], w_sem.at[0, c]),
            pltpu.make_async_copy(wu_hbm.at[:, span(c)], w_pair.at[c, :, pl.ds(chunk, chunk)], w_sem.at[1, c]),
            pltpu.make_async_copy(wd_hbm.at[span(c), :], w_low.at[c], w_sem.at[2, c]),
        )

    def results(c):
        return [
            pltpu.make_async_copy(acts.at[c, :, k], outs[k].at[:, :, span(c)], out_sem.at[k, c])
            for k in range(3)
        ]

    def remote(stage, c):
        source, target, device = (
            (send1.at[c], recv1.at[c], near_x),
            (send2.at[c], recv2.at[c], near_y),
            (acts.at[c, me], acts.at[c, me], near_x),
            (acts.at[c, pl.ds(2 * y, 2)], acts.at[c, pl.ds(2 * y, 2)], near_y),
        )[stage]
        return pltpu.make_async_remote_copy(
            src_ref=source, dst_ref=target, send_sem=ssem.at[stage, c], recv_sem=rsem.at[stage, c],
            device_id={"fsdp": device}, device_id_type=MESH,
        )

    @pl.loop(0, n)
    def _(c):
        for copy in weights(c):
            copy.start()

    barrier = pltpu.get_barrier_semaphore()
    for device in (near_x, near_y):
        pl.semaphore_signal(barrier, inc=1, device_id={"fsdp": device}, device_id_type=MESH)
    pl.semaphore_wait(barrier, 2)

    total[...] = jnp.zeros_like(total)

    @pl.loop(0, n + 4 * LAG)
    def _(step):
        @pl.when(step < n)
        def _():
            c = step
            slot = lax.rem(c, slots)
            for copy in weights(c):
                copy.wait()
            pair = jnp.dot(x_ref[...], w_pair[c], preferred_element_type=F32)
            part[slot, :, 0] = pair[:, :chunk].reshape(4, -1, chunk)
            part[slot, :, 1] = pair[:, chunk:].reshape(4, -1, chunk)
            part[slot, :, 2] = dot_dims(dy_ref[...], w_low[c], 1, 1).reshape(4, -1, chunk)
            for row in range(2):
                send1[c, row] = part[slot, 2 * row + 1 - x].astype(BF16)
            remote(0, c).start()

        @pl.when((step >= LAG) & (step < n + LAG))
        def _():
            c = step - LAG
            slot = lax.rem(c, slots)
            remote(0, c).wait_recv()
            send2[c] = (part[slot, near_y] + recv1[c, 1 - y].astype(F32)).astype(BF16)
            remote(1, c).start()

        @pl.when((step >= 2 * LAG) & (step < n + 2 * LAG))
        def _():
            c = step - 2 * LAG
            slot = lax.rem(c, slots)
            remote(1, c).wait_recv()
            sums = [
                part[slot, me, k] + recv1[c, y, k].astype(F32) + recv2[c, k].astype(F32)
                for k in range(3)
            ]
            for k, value in enumerate(activations(*sums)):
                acts[c, me, k] = value
            remote(2, c).start()

        @pl.when((step >= 3 * LAG) & (step < n + 3 * LAG))
        def _():
            c = step - 3 * LAG
            remote(2, c).wait_recv()
            remote(3, c).start()

        @pl.when(step >= 4 * LAG)
        def _():
            c = step - 4 * LAG
            remote(3, c).wait_recv()
            for copy in results(c):
                copy.start()
            pair = jnp.concatenate(
                [acts[c, :, 1].reshape(-1, chunk), acts[c, :, 2].reshape(-1, chunk)], axis=1
            )
            total[...] += dot_dims(pair, w_pair[c], 1, 1)
            for stage in range(4):
                remote(stage, c).wait_send()

    @pl.loop(0, n)
    def _(c):
        for copy in results(c):
            copy.wait()


def middle_fused(x_block, dy_block, w_gate, w_up, w_down):
    tokens, width = x_block.shape
    units = w_gate.shape[1]
    chunk = 128
    n, rows = units // chunk, tokens // 4
    whole, anywhere = pl.BlockSpec(memory_space=pltpu.VMEM), pl.BlockSpec(memory_space=pl.ANY)
    wide = jax.ShapeDtypeStruct((4, rows, units), BF16)
    *acts, total = pl.pallas_call(
        functools.partial(middle_kernel, n),
        out_shape=(wide, wide, wide, jax.ShapeDtypeStruct((tokens, width), F32)),
        in_specs=[whole, whole, anywhere, anywhere, anywhere],
        out_specs=(anywhere, anywhere, anywhere, whole),
        scratch_shapes=[
            pltpu.VMEM((n, width, 2 * chunk), BF16),
            pltpu.VMEM((n, chunk, width), BF16),
            pltpu.VMEM((2 * LAG + 1, 4, 3, rows, chunk), F32),
            pltpu.VMEM((n, 2, 3, rows, chunk), BF16),
            pltpu.VMEM((n, 2, 3, rows, chunk), BF16),
            pltpu.VMEM((n, 3, rows, chunk), BF16),
            pltpu.VMEM((n, 3, rows, chunk), BF16),
            pltpu.VMEM((n, 4, 3, rows, chunk), BF16),
            pltpu.SemaphoreType.DMA((3, n)),
            pltpu.SemaphoreType.DMA((3, n)),
            pltpu.SemaphoreType.DMA((4, n)),
            pltpu.SemaphoreType.DMA((4, n)),
        ],
        compiler_params=pltpu.CompilerParams(
            collective_id=0, has_side_effects=True, vmem_limit_bytes=60 * 2**20
        ),
        cost_estimate=pl.CostEstimate(
            flops=10 * tokens * width * units, bytes_accessed=12 * width * units, transcendentals=0
        ),
    )(x_block, dy_block, w_gate, w_up, w_down)
    return (*[v.reshape(tokens, units) for v in acts], total)


def scatter_tokens(partial, n_rep, n_fsdp):
    rows, width = partial.shape
    halves = n_rep // n_fsdp
    pieces = partial.reshape(n_fsdp, rows // n_fsdp, halves, width // halves)
    pieces = pieces.transpose(0, 2, 1, 3).reshape(n_rep, rows // n_fsdp, width // halves)
    piece = lax.psum_scatter(pieces, "rep", scatter_dimension=0, tiled=False)
    pairs = []
    for f in range(n_fsdp):
        for r in range(n_rep):
            t, h = divmod(r, halves)
            pairs.append((r * n_fsdp + f, (f * halves + h) * n_fsdp + t))
    return lax.ppermute(piece.astype(BF16), ("rep", "fsdp"), pairs)


def solution(mesh):
    n_rep, n_fsdp = mesh.shape["rep"], mesh.shape["fsdp"]

    def body(tokens, grad_out, w_gate, w_up, w_down):
        x_block, dy_block = gather_blocks(tokens, grad_out)
        middle = middle_fused if n_fsdp == 4 else middle_plain
        hidden, d_gate, d_up, partial = middle(x_block, dy_block, w_gate, w_up, w_down)
        grad_tokens = scatter_tokens(partial, n_rep, n_fsdp)
        x_turned, dy_turned = rotate_features(x_block), rotate_features(dy_block)
        return (
            grad_tokens,
            dot_dims(x_turned, d_gate, 0, 0).astype(BF16),
            dot_dims(x_turned, d_up, 0, 0).astype(BF16),
            dot_dims(hidden, dy_turned, 0, 0).astype(BF16),
        )

    return jax.shard_map(
        body,
        mesh=mesh,
        in_specs=(P("fsdp", "rep"),) * 4 + (P("rep", "fsdp"),),
        out_specs=(P("fsdp", "rep"),) * 3 + (P("rep", "fsdp"),),
        check_vma=False,
    )
```

time: 1010 us -> 316 us (0.31)
  waiting for transfers between devices: 815 us -> 54.2 us
  Pallas kernels: 0 us -> 176 us
  matrix products: 142 us -> 20 us
  blocking collectives: 16.3 us -> 28.8 us
    all_gather x8 -> x1, waiting for transfers between devices: 799 us -> 31.6 us  [gather_blocks(): full = lax.all_gather(both, 'rep', axis=2, tiled=True)]
    pallas_call x0 -> x1, Pallas kernels: none -> 176 us  [middle_fused(): pl.pallas_call(functools.partial(middle_kernel, n), out_shape=(wide, wide...]
    dot_general x11 -> x5, matrix products: 142 us -> 20 us  [the longest x3 17.9 us: dot_dims(): lax.dot_general(left, right, (((left_dim,), (right_dim,)), ((), ())), pre...]
    reduce_scatter x1, waiting for transfers between devices: 0.01 us -> 20.9 us  [scatter_tokens(): piece = lax.psum_scatter(pieces, 'rep', scatter_dimension=0, tiled=False)]
    all_to_all x1, blocking collectives: 16.3 us -> 28.8 us  [gather_blocks(): lax.all_to_all(full, 'fsdp', split_axis=2, concat_axis=1, tiled=True)]
    all_to_all x1 -> x0, waiting for transfers between devices: 11.5 us -> none  [body(): lax.all_to_all(dy_full, 'fsdp', split_axis=1, concat_axis=0, tiled=True)]
  transfers between devices with their start and end apart: 10 -> 3, of which waited for: 9 -> 3; matrix products, arithmetic and copies ran while one was open for 7% -> 7% of each run, Pallas kernels for 0% -> 0%
where the time goes in v1:
time: 316 us
  Pallas kernels  176 us (56%)
  waiting for transfers between devices  54.2 us (17%)
  blocking collectives  28.8 us (9%)
  matrix products  20 us (6%)
  local copies, waits for them, and re-layouts  17.9 us (6%)
  between operations  14.1 us (4%)
    pallas_call x1, Pallas kernels, middle_fused(): pl.pallas_call(functools.partial(middle_kernel, n), out_shape=(wide, wide...  176 us
    all_gather x1, waiting for transfers between devices, gather_blocks(): full = lax.all_gather(both, 'rep', axis=2, tiled=True)  31.6 us
    all_to_all x1, blocking collectives, gather_blocks(): lax.all_to_all(full, 'fsdp', split_axis=2, concat_axis=1, tiled=True)  28.8 us
    reduce_scatter x1, waiting for transfers between devices, scatter_tokens(): piece = lax.psum_scatter(pieces, 'rep', scatter_dimension=0, tiled=False)  20.9 us
    dot_general x3, matrix products, dot_dims(): lax.dot_general(left, right, (((left_dim,), (right_dim,)), ((), ())), pre...  17.9 us
  transfers between devices with their start and end apart: 3, of which 3 were waited for; matrix products, arithmetic and copies ran while one was open for 7% of the time, Pallas kernels for 0%

profile of v1, /device:TPU:2, one launch (start us, length us, event | category | flops | bytes accessed | tf_op | source)
XLA Modules:
  0.0 315.5 jit_solution(681990659244818430)
XLA Ops:
  7.2 0.0 all-gather.2.cloned.1.call-start
  7.2 1.7 pad_maximum_fusion
  8.9 0.0 all-gather.2.cloned.1.call-update
  8.9 0.0 reduce-scatter.2.cloned.1.call-start
  9.0 31.6 %all-gather.2.cloned.1.call-done = bf16[2,128,4096]{2,1,0:T(8,128)(2,1)} async-done(((bf16[2,128,512]{2,1,0:T(8,128)(2,1)}), bf16[2,128,4096]{2,1,0:T(8,128)(2,1)}) %all-gather.2.cloned.1.call-update) | async-done | bytes 2097168 | tf_op jit(solution)/shard_map/all_gather | solution.py:40
  40.5 4.7 %copy.21 = bf16[2,128,4096]{1,0,2:T(2,128)(2,1)S(1)} copy(bf16[2,128,4096]{2,1,0:T(8,128)(2,1)} %all-gather.2.cloned.1.call-done) | data formatting | bytes 4194304 | tf_op jit(solution)/shard_map/all_gather | solution.py:40
  45.3 28.8 %all_to_all.15 = bf16[2,128,4096]{1,0,2:T(2,128)(2,1)} all-to-all(bf16[2,128,4096]{1,0,2:T(2,128)(2,1)S(1)} %copy.21), channel_id=1, replica_groups=mesh['rep'=8,'fsdp'=4] {'fsdp'}, dimensions={2} | all-to-all | bytes 4194304 | tf_op jit(solution)/shard_map/all_to_all | solution.py:41
  74.0 4.7 %copy.22 = bf16[2,128,4,1024]{3,1,2,0:T(8,128)(2,1)S(1)} copy(bf16[2,128,4,1024]{1,0,3,2:T(2,128)(2,1)} %bitcast.35) | data formatting | bytes 4194304 | tf_op jit(solution)/shard_map/all_to_all | solution.py:41
  78.8 1.6 fusion.42
  80.4 175.8 %shard_map.84 = (bf16[4,128,3072]{2,1,0:T(8,128)(2,1)}, bf16[4,128,3072]{2,1,0:T(8,128)(2,1)}, bf16[4,128,3072]{2,1,0:T(8,128)(2,1)}, f32[512,1024]{1,0:T(8,128)}) custom-call(bf16[512,1024]{1,0:T(8,128)(2,1)} %bitcast.41, bf16[512,1024]{1,0:T(8,128)(2,1)} %bitcast.39, bf16[1024,3072]{1,0:T(8,128)(2,1)} %wg_hbm.1, bf16[1024,3072]{1,0:T(8,128)(2,1)} %wu_hbm.1, ...), custom_call_target="tpu_custom_call" | custom-call | flops 16106127360 | bytes 37748736 | tf_op jit(solution)/shard_map/pallas_call | solution.py:194
  256.2 3.0 reshape.41
  259.2 0.0 copy-start.1
  259.3 1.7 copy.23
  261.0 0.0 copy-start
  261.0 0.0 reduce-scatter.2.cloned.1.call-update
  261.0 0.0 copy-done.1
  261.0 0.3 copy.26
  261.3 0.9 copy-done
  262.2 0.0 copy-start.3
  262.2 0.3 copy.27
  262.5 1.1 convolution_convert_fusion.4
  263.5 1.1 convolution_convert_fusion.3
  264.6 0.0 copy-done.3
  264.6 0.0 copy-start.2
  264.6 5.3 %convolution_convert_fusion.2 = bf16[1024,3072]{1,0:T(8,128)(2,1)} fusion(bf16[512,1024]{0,1:T(8,128)(2,1)S(1)} %bitcast.44, bf16[512,3072]{1,0:T(8,128)(2,1)S(1)} %bitcast.50), kind=kOutput, calls=%fused_computation.2 | convolution fusion | flops 3224371200 | bytes 10485760 | tf_op jit(solution)/shard_map/dot_general | solution.py:26
  269.9 0.0 copy-done.2
  269.9 5.3 %convolution_convert_fusion.1 = bf16[1024,3072]{1,0:T(8,128)(2,1)} fusion(bf16[512,1024]{0,1:T(8,128)(2,1)S(1)} %bitcast.45, bf16[512,3072]{1,0:T(8,128)(2,1)S(1)} %bitcast.49), kind=kOutput, calls=%fused_computation.1 | convolution fusion | flops 3224371200 | bytes 10485760 | tf_op jit(solution)/shard_map/dot_general | solution.py:26
  275.2 20.9 %reduce-scatter.2.cloned.1.call-done = f32[1,128,512]{2,1,0:T(8,128)} async-done(((f32[8,128,512]{2,1,0:T(8,128)}), f32[1,128,512]{2,1,0:T(8,128)}) %reduce-scatter.2.cloned.1.call-update) | async-done | bytes 262160 | tf_op jit(solution)/shard_map/reduce_scatter | solution.py:228
  296.1 1.0 convert_bitcast_fusion
  297.1 1.9 collective-permute-start
  299.0 7.3 %convolution_convert_fusion = bf16[3072,1024]{1,0:T(8,128)(2,1)} fusion(bf16[512,3072]{1,0:T(8,128)(2,1)} %bitcast.48, bf16[512,1024]{0,1:T(8,128)(2,1)S(1)} %bitcast.43), kind=kOutput, calls=%fused_computation | convolution fusion | flops 3224371200 | bytes 10485760 | tf_op jit(solution)/shard_map/dot_general | solution.py:26
  306.3 1.7 collective-permute-done
  308.0 0.7 copy.33
Async XLA Ops:
  7.2 33.4 %all-gather.2.cloned.1.call-start = ((), (), s32[]{:S(2)}) async-start(), calls=%async_computation.2 | async-start | bytes 2359296 | tf_op jit(solution)/shard_map/all_gather | solution.py:40
  8.9 287.2 %reduce-scatter.2.cloned.1.call-start = ((), (), s32[]{:S(2)}) async-start(), calls=%async_computation.3 | async-start | bytes 2359296 | tf_op jit(solution)/shard_map/reduce_scatter | solution.py:228
  259.2 1.7 copy-start.1
  261.0 1.2 copy-start
  262.2 2.4 copy-start.3
  264.6 5.3 %copy-start.2 = (bf16[4,128,3072]{2,1,0:T(8,128)(2,1)S(1)}, bf16[4,128,3072]{2,1,0:T(8,128)(2,1)}, u32[]{:S(2)}) copy-start(bf16[4,128,3072]{2,1,0:T(8,128)(2,1)} %get-tuple-element.10) | copy-start | bytes 9437188
  297.1 10.9 %collective-permute-start = (bf16[128,512]{1,0:T(8,128)(2,1)S(1)}, bf16[128,512]{1,0:T(8,128)(2,1)S(1)}, u32[]{:S(2)}, u32[]{:S(2)}) collective-permute-start(bf16[128,512]{1,0:T(8,128)(2,1)S(1)} %convert_bitcast_fusion), channel_id=1, source_target_pairs={{0,0},{4,4},{8,1},{12,5},{16,2},{20,6},{24,3},{28,7},{1,8},{5,12},... | collective-permute-start | bytes 393224 | tf_op jit(solution)/shard_map/ppermute | solution.py:234
Sparse Core Ops, SparseCore 0:
  10.2 30.3 all-gather.1
  261.1 34.9 reduce-scatter.1

commit v2 on v1

v2 whole, which is shorter than its diff:
```python
import functools
import math

import jax
import jax.numpy as jnp
from jax import lax
from jax.experimental import pallas as pl
from jax.experimental.pallas import tpu as pltpu
from jax.sharding import PartitionSpec as P

HB = 128
BF16 = jnp.bfloat16
F32 = jnp.float32


def hadamard(size):
    index = jnp.arange(size, dtype=jnp.int32)
    both = index[:, None] & index[None, :]
    parity = jnp.zeros((size, size), jnp.int32)
    for bit_pos in range(size.bit_length() - 1):
        parity = parity + (both >> bit_pos & 1)
    return (1 - 2 * (parity % 2)).astype(F32) / math.sqrt(size)


def dot_dims(left, right, left_dim, right_dim, kind=F32):
    return lax.dot_general(
        left, right, (((left_dim,), (right_dim,)), ((), ())), preferred_element_type=kind
    )


def rotate_features(block):
    rows, width = block.shape
    parts = block.astype(F32).reshape(rows, width // HB, HB)
    turned = jnp.einsum("tbj,ij->tbi", parts, hadamard(HB), precision=lax.Precision.HIGHEST)
    return turned.reshape(rows, width).astype(BF16)


def gather_blocks(tokens, grad_out):
    both = jnp.stack([tokens, grad_out])
    full = lax.all_gather(both, "rep", axis=2, tiled=True)
    block = lax.all_to_all(full, "fsdp", split_axis=2, concat_axis=1, tiled=True)
    return block[0], block[1]


def activations(gate, up, d_hidden):
    sig = jax.nn.sigmoid(gate)
    active = gate * sig
    hidden = (active * up).astype(BF16)
    d_gate = (d_hidden * up * sig * (1.0 + gate * (1.0 - sig))).astype(BF16)
    d_up = (d_hidden * active).astype(BF16)
    return hidden, d_gate, d_up


def middle_plain(x_block, dy_block, w_gate, w_up, w_down):
    sums = [
        lax.psum_scatter(part, "fsdp", scatter_dimension=0, tiled=True)
        for part in (
            dot_dims(x_block, w_gate, 1, 0),
            dot_dims(x_block, w_up, 1, 0),
            dot_dims(dy_block, w_down, 1, 1),
        )
    ]
    own = activations(*sums)
    hidden, d_gate, d_up = [lax.all_gather(v, "fsdp", axis=0, tiled=True) for v in own]
    partial = dot_dims(d_gate, w_gate, 1, 1) + dot_dims(d_up, w_up, 1, 1)
    return hidden, d_gate, d_up, partial


def scatter_tokens(partial, n_rep, n_fsdp):
    rows, width = partial.shape
    halves = n_rep // n_fsdp
    pieces = partial.reshape(n_fsdp, rows // n_fsdp, halves, width // halves)
    pieces = pieces.transpose(0, 2, 1, 3).reshape(n_rep, rows // n_fsdp, width // halves)
    piece = lax.psum_scatter(pieces, "rep", scatter_dimension=0, tiled=False)
    pairs = []
    for f in range(n_fsdp):
        for r in range(n_rep):
            t, h = divmod(r, halves)
            pairs.append((r * n_fsdp + f, (f * halves + h) * n_fsdp + t))
    return lax.ppermute(piece.astype(BF16), ("rep", "fsdp"), pairs)


MESH = pl.DeviceIdType.MESH
LAG = 2


def fused_kernel(
    n, tok_ref, go_ref, sign_ref, wg_hbm, wu_hbm, wd_hbm,
    hid_out, dg_out, du_out, gt_out, xt_out, dyt_out,
    w_pair, w_low, part, send1, recv1, send2, recv2, acts, hid,
    zbuf, gath, x_ref, dy_ref, total, e1recv, e2send, e2recv, e3send, e3recv,
    w_sem, out_sem, ssem, rsem, gs_sem, gr_sem, hs_sem, hr_sem, es_sem, er_sem,
):
    chunk = w_low.shape[1]
    slots = part.shape[0]
    rows, feats = tok_ref.shape
    me, rep = lax.axis_index("fsdp"), lax.axis_index("rep")
    z, h = rep // 2, rep % 2
    sibling = rep + 1 - 2 * h
    y, x = me // 2, me % 2
    near_x, near_y, far = 2 * y + 1 - x, 2 * (1 - y) + x, 3 - me

    def span(c, size):
        return pl.ds(pl.multiple_of(c * size, size), size)

    def send(source, target, send_sem, recv_sem, fsdp, to):
        return pltpu.make_async_remote_copy(
            src_ref=source, dst_ref=target, send_sem=send_sem, recv_sem=recv_sem,
            device_id={"rep": to, "fsdp": fsdp}, device_id_type=MESH,
        )

    def weights(c):
        columns = span(c, chunk)
        return (
            pltpu.make_async_copy(wg_hbm.at[:, columns], w_pair.at[c, :, pl.ds(0, chunk)], w_sem.at[0, c]),
            pltpu.make_async_copy(wu_hbm.at[:, columns], w_pair.at[c, :, pl.ds(chunk, chunk)], w_sem.at[1, c]),
            pltpu.make_async_copy(wd_hbm.at[columns, :], w_low.at[c], w_sem.at[2, c]),
        )

    def results(c):
        return [
            pltpu.make_async_copy(acts.at[c, :, k], out.at[:, :, span(c, chunk)], out_sem.at[k, c])
            for k, out in enumerate((dg_out, du_out))
        ]

    def hidden_result(c):
        return pltpu.make_async_copy(hid.at[c], hid_out.at[:, :, span(c, chunk)], out_sem.at[2, c])

    def partners(c):
        odd = lax.rem(c, 2)
        first = near_x * (1 - odd) + near_y * odd
        return first, near_x + near_y - first

    def remote(stage, c):
        first, second = partners(c)
        source, target, device = (
            (send1.at[c, 0], recv1.at[c, 0], first),
            (send1.at[c, 1], recv1.at[c, 1], first),
            (send2.at[c], recv2.at[c], second),
            (acts.at[c, me], acts.at[c, me], first),
            (acts.at[c, me], acts.at[c, me], second),
            (acts.at[c, first], acts.at[c, first], second),
        )[stage]
        return send(source, target, ssem.at[stage, c], rsem.at[stage, c], device, rep)

    @pl.loop(0, n)
    def _(c):
        for copy in weights(c):
            copy.start()

    zbuf[z, 0] = tok_ref[...]
    zbuf[z, 1] = go_ref[...]

    barrier = pltpu.get_barrier_semaphore()

    def greet(fsdp, to):
        pl.semaphore_signal(
            barrier, inc=1, device_id={"rep": to, "fsdp": fsdp}, device_id_type=MESH
        )

    for k in range(1, 4):
        greet(me, 2 * ((z + k) % 4) + h)
        greet((me + k) % 4, rep)
    greet(me, sibling)

    @pl.when(me != z)
    def _():
        greet(z, 2 * me + h)

    pl.semaphore_wait(barrier, 7 + jnp.where(me != z, 1, 0))

    def along_z(k):
        return send(zbuf.at[z], zbuf.at[z], gs_sem.at[0, k], gr_sem.at[0, z], me, 2 * ((z + k) % 4) + h)

    def to_owner(block):
        return send(zbuf.at[block], gath.at[me, h], gs_sem.at[1, block], gr_sem.at[1, me], block, rep)

    def to_core(owner):
        return send(gath.at[owner, h], gath.at[owner, h], gs_sem.at[2, owner], gr_sem.at[2, owner], me, sibling)

    def arrived(target, sem):
        pltpu.make_async_copy(target, target, sem).wait()

    def pass_on(block):
        @pl.when(block != me)
        def _():
            to_owner(block).start()

        @pl.when(block == me)
        def _():
            gath[me, h] = zbuf[block]
            to_core(me).start()

    for k in (1, 3, 2):
        along_z(k).start()
    pass_on(z)
    for k in (1, 3, 2):
        block = (z + k) % 4
        arrived(zbuf.at[block], gr_sem.at[0, block])
        pass_on(block)
    for k in (1, 2, 3):
        owner = (me + k) % 4
        arrived(gath.at[owner, h], gr_sem.at[1, owner])
        to_core(owner).start()
    for k in range(4):
        owner = (me + k) % 4
        arrived(gath.at[owner, 1 - h], gr_sem.at[2, owner])
    for owner in range(4):
        for half in range(2):
            place = (pl.ds(owner * rows, rows), pl.ds(half * feats, feats))
            x_ref[place] = gath[owner, half, 0]
            dy_ref[place] = gath[owner, half, 1]

    total[...] = jnp.zeros_like(total)

    @pl.loop(0, n + 4 * LAG)
    def _(step):
        @pl.when(step < n)
        def _():
            c = step
            slot = lax.rem(c, slots)
            for copy in weights(c):
                copy.wait()
            pair = jnp.dot(x_ref[...], w_pair[c], preferred_element_type=F32)
            part[slot, :, 0] = pair[:, :chunk].reshape(4, -1, chunk)
            part[slot, :, 1] = pair[:, chunk:].reshape(4, -1, chunk)
            part[slot, :, 2] = dot_dims(dy_ref[...], w_low[c], 1, 1).reshape(4, -1, chunk)
            first, _ = partners(c)
            send1[c, 0] = part[slot, far].astype(BF16)
            remote(0, c).start()
            send1[c, 1] = part[slot, first].astype(BF16)
            remote(1, c).start()

        @pl.when((step >= LAG) & (step < n + LAG))
        def _():
            c = step - LAG
            slot = lax.rem(c, slots)
            _, second = partners(c)
            remote(0, c).wait_recv()
            send2[c] = (part[slot, second] + recv1[c, 0].astype(F32)).astype(BF16)
            remote(2, c).start()

        @pl.when((step >= 2 * LAG) & (step < n + 2 * LAG))
        def _():
            c = step - 2 * LAG
            slot = lax.rem(c, slots)
            remote(1, c).wait_recv()
            remote(2, c).wait_recv()
            sums = [
                part[slot, me, k] + recv1[c, 1, k].astype(F32) + recv2[c, k].astype(F32)
                for k in range(3)
            ]
            hidden, d_gate, d_up = activations(*sums)
            acts[c, me, 0] = d_gate
            acts[c, me, 1] = d_up
            remote(3, c).start()
            remote(4, c).start()
            hid[c, me] = hidden

        @pl.when((step >= 3 * LAG) & (step < n + 3 * LAG))
        def _():
            c = step - 3 * LAG
            remote(3, c).wait_recv()
            remote(5, c).start()

        @pl.when(step >= 4 * LAG)
        def _():
            c = step - 4 * LAG
            remote(4, c).wait_recv()
            remote(5, c).wait_recv()
            for copy in results(c):
                copy.start()
            pair = jnp.concatenate(
                [acts[c, :, 0].reshape(-1, chunk), acts[c, :, 1].reshape(-1, chunk)], axis=1
            )
            total[...] += dot_dims(pair, w_pair[c], 1, 1)
            for stage in range(6):
                remote(stage, c).wait_send()

    low, high = pl.ds(0, n // 2), pl.ds(n // 2, n - n // 2)

    def hidden_copy(k):
        part_of, owner, device = (
            (low, me, near_x), (high, me, near_y), (high, me, near_x), (low, me, near_y),
            (low, near_x, near_y), (high, near_y, near_x),
        )[k]
        block = hid.at[part_of, owner]
        return send(block, block, hs_sem.at[k], hr_sem.at[k], device, rep)

    for k in range(4):
        hidden_copy(k).start()

    def half(core):
        return pl.ds(pl.multiple_of(core * feats, feats), feats)

    fold = send(total.at[:, half(1 - h)], e1recv, es_sem.at[0], er_sem.at[0], me, sibling)
    fold.start()
    scale = 1.0 / math.sqrt(HB)
    for source, target in ((x_ref, xt_out), (dy_ref, dyt_out)):
        for b in range(source.shape[1] // HB):
            columns = pl.ds(b * HB, HB)
            turned = jnp.dot(source[:, columns], sign_ref[...], preferred_element_type=F32)
            target[:, columns] = (turned * scale).astype(BF16)
    fold.wait()
    for t in range(4):
        block = pl.ds(t * rows, rows)
        e1recv[block, :] = e1recv[block, :] + total[block, half(h)]
        e2send[t] = e1recv[block, :].astype(BF16)

    def piece(k):
        t = (z + k) % 4
        return send(e2send.at[t], e2recv.at[z], es_sem.at[k], er_sem.at[1 + z], me, 2 * t + h)

    for k in (2, 1, 3):
        piece(k).start()
    hidden_copy(0).wait_recv()
    hidden_copy(4).start()
    hidden_copy(1).wait_recv()
    hidden_copy(5).start()
    for k in (1, 3, 2):
        source = (z + k) % 4
        arrived(e2recv.at[source], er_sem.at[1 + source])
    mine = e1recv[span(z, rows), :]
    for k in range(1, 4):
        mine = mine + e2recv[(z + k) % 4].astype(F32)
    e3send[...] = mine.astype(BF16)
    swap = send(e3send, e3recv, es_sem.at[4], er_sem.at[5], z, 2 * me + h)

    @pl.when(me != z)
    def _():
        swap.start()
        swap.wait()
        gt_out[...] = e3recv[...]

    @pl.when(me == z)
    def _():
        gt_out[...] = e3send[...]

    for k in range(2, 6):
        hidden_copy(k).wait_recv()

    @pl.loop(0, n)
    def _(c):
        hidden_result(c).start()

    for k in range(6):
        hidden_copy(k).wait_send()
    for k in range(1, 4):
        piece(k).wait_send()
        along_z(k).wait_send()
    for block in range(4):
        @pl.when(block != me)
        def _():
            to_owner(block).wait_send()

        to_core(block).wait_send()

    @pl.loop(0, n)
    def _(c):
        for copy in results(c):
            copy.wait()
        hidden_result(c).wait()


def fused(tokens, grad_out, w_gate, w_up, w_down):
    rows, feats = tokens.shape
    width, units = w_gate.shape
    chunk = 128
    n, count = units // chunk, 4 * rows
    signs = (hadamard(HB) * math.sqrt(HB)).astype(BF16)
    whole, anywhere = pl.BlockSpec(memory_space=pltpu.VMEM), pl.BlockSpec(memory_space=pl.ANY)
    wide = jax.ShapeDtypeStruct((4, rows, units), BF16)
    turned = jax.ShapeDtypeStruct((count, width), BF16)
    dma = pltpu.SemaphoreType.DMA
    hidden, d_gate, d_up, grad_tokens, x_turned, dy_turned = pl.pallas_call(
        functools.partial(fused_kernel, n),
        out_shape=(wide, wide, wide, jax.ShapeDtypeStruct((rows, feats), BF16), turned, turned),
        in_specs=[whole] * 3 + [anywhere] * 3,
        out_specs=(anywhere,) * 3 + (whole,) * 3,
        scratch_shapes=[
            pltpu.VMEM((n, width, 2 * chunk), BF16),
            pltpu.VMEM((n, chunk, width), BF16),
            pltpu.VMEM((2 * LAG + 1, 4, 3, rows, chunk), F32),
            pltpu.VMEM((n, 2, 3, rows, chunk), BF16),
            pltpu.VMEM((n, 2, 3, rows, chunk), BF16),
            pltpu.VMEM((n, 3, rows, chunk), BF16),
            pltpu.VMEM((n, 3, rows, chunk), BF16),
            pltpu.VMEM((n, 4, 2, rows, chunk), BF16),
            pltpu.VMEM((n, 4, rows, chunk), BF16),
            pltpu.VMEM((4, 2, rows, feats), BF16),
            pltpu.VMEM((4, 2, 2, rows, feats), BF16),
            pltpu.VMEM((count, width), BF16),
            pltpu.VMEM((count, width), BF16),
            pltpu.VMEM((count, width), F32),
            pltpu.VMEM((count, feats), F32),
            pltpu.VMEM((4, rows, feats), BF16),
            pltpu.VMEM((4, rows, feats), BF16),
            pltpu.VMEM((rows, feats), BF16),
            pltpu.VMEM((rows, feats), BF16),
            dma((3, n)), dma((3, n)), dma((6, n)), dma((6, n)),
            dma((3, 4)), dma((3, 4)), dma((6,)), dma((6,)), dma((5,)), dma((6,)),
        ],
        compiler_params=pltpu.CompilerParams(
            collective_id=0, has_side_effects=True, vmem_limit_bytes=62 * 2**20
        ),
        cost_estimate=pl.CostEstimate(
            flops=10 * count * width * units, bytes_accessed=12 * width * units, transcendentals=0
        ),
    )(tokens, grad_out, signs, w_gate, w_up, w_down)
    flat = [v.reshape(count, units) for v in (hidden, d_gate, d_up)]
    return (*flat, grad_tokens, x_turned, dy_turned)


def plain(n_rep, n_fsdp, tokens, grad_out, w_gate, w_up, w_down):
    x_block, dy_block = gather_blocks(tokens, grad_out)
    hidden, d_gate, d_up, partial = middle_plain(x_block, dy_block, w_gate, w_up, w_down)
    grad_tokens = scatter_tokens(partial, n_rep, n_fsdp)
    return hidden, d_gate, d_up, grad_tokens, rotate_features(x_block), rotate_features(dy_block)


def solution(mesh):
    n_rep, n_fsdp = mesh.shape["rep"], mesh.shape["fsdp"]
    whole = fused if (n_rep, n_fsdp) == (8, 4) else functools.partial(plain, n_rep, n_fsdp)

    def body(tokens, grad_out, w_gate, w_up, w_down):
        hidden, d_gate, d_up, grad_tokens, x_turned, dy_turned = whole(
            tokens, grad_out, w_gate, w_up, w_down
        )
        return (
            grad_tokens,
            dot_dims(x_turned, d_gate, 0, 0).astype(BF16),
            dot_dims(x_turned, d_up, 0, 0).astype(BF16),
            dot_dims(hidden, dy_turned, 0, 0).astype(BF16),
        )

    return jax.shard_map(
        body,
        mesh=mesh,
        in_specs=(P("fsdp", "rep"),) * 4 + (P("rep", "fsdp"),),
        out_specs=(P("fsdp", "rep"),) * 3 + (P("rep", "fsdp"),),
        check_vma=False,
    )
```

time: 316 us -> 235 us (0.74)
  waiting for transfers between devices: 54.2 us -> 0 us
  Pallas kernels: 176 us -> 214 us
  blocking collectives: 28.8 us -> 0 us
  local copies, waits for them, and re-layouts: 17.9 us -> 0.68 us
  between operations: 14.1 us -> 0.67 us
    pallas_call x1, Pallas kernels: 176 us -> 214 us  [fused(): pl.pallas_call(functools.partial(fused_kernel, n), out_shape=(wide, wide,...]
    all_gather x1 -> x0, waiting for transfers between devices: 31.6 us -> none  [gather_blocks(): full = lax.all_gather(both, 'rep', axis=2, tiled=True)]
    all_to_all x1 -> x0, blocking collectives: 28.8 us -> none  [gather_blocks(): lax.all_to_all(full, 'fsdp', split_axis=2, concat_axis=1, tiled=True)]
    reduce_scatter x1 -> x0, waiting for transfers between devices: 20.9 us -> none  [scatter_tokens(): piece = lax.psum_scatter(pieces, 'rep', scatter_dimension=0, tiled=False)]
    all_to_all x1 -> x0, local copies, waits for them, and re-layouts: 4.73 us -> none  [gather_blocks(): lax.all_to_all(full, 'fsdp', split_axis=2, concat_axis=1, tiled=True)]
    all_gather x1 -> x0, local copies, waits for them, and re-layouts: 4.72 us -> none  [gather_blocks(): full = lax.all_gather(both, 'rep', axis=2, tiled=True)]
  transfers between devices with their start and end apart: 3 -> 0, of which waited for: 3 -> 0; matrix products, arithmetic and copies ran while one was open for 7% -> 0% of each run, Pallas kernels for 0% -> 0%
where the time goes in v2:
time: 235 us
  Pallas kernels  214 us (91%)
  matrix products  19.3 us (8%)
    pallas_call x1, Pallas kernels, fused(): pl.pallas_call(functools.partial(fused_kernel, n), out_shape=(wide, wide,...  214 us
    dot_general x3, matrix products, dot_dims(): lax.dot_general(left, right, (((left_dim,), (right_dim,)), ((), ())), pre...  19.3 us

profile of v2, /device:TPU:2, one launch (start us, length us, event | category | flops | bytes accessed | tf_op | source)
XLA Modules:
  0.0 235.3 jit_solution(17214627259899834098)
XLA Ops:
  0.6 0.7 fusion.5.sign_ref
  1.3 214.0 %shard_map.84 = (bf16[4,128,3072]{2,1,0:T(8,128)(2,1)}, bf16[4,128,3072]{2,1,0:T(8,128)(2,1)}, bf16[4,128,3072]{2,1,0:T(8,128)(2,1)}, bf16[128,512]{1,0:T(8,128)...) custom-call(bf16[128,512]{1,0:T(8,128)(2,1)} %tok_ref.1, bf16[128,512]{1,0:T(8,128)(2,1)} %go_ref.1, ...), custom_call_target="tpu_custom_call" | custom-call | flops 16106127360 | bytes 37748736 | tf_op jit(solution)/shard_map/pallas_call | solution.py:375
  215.3 0.0 copy-start.2
  215.3 0.0 copy-start.3
  215.3 8.5 %convolution_convert_fusion.2 = bf16[1024,3072]{1,0:T(8,128)(2,1)} fusion(bf16[512,1024]{1,0:T(8,128)(2,1)} %get-tuple-element.11, bf16[512,3072]{1,0:T(8,128)(2,1)} %bitcast.11), kind=kOutput, calls=%fused_computation.2 | convolution fusion | flops 3224371200 | bytes 10485760 | tf_op jit(solution)/shard_map/dot_general | solution.py:26
  223.9 0.0 copy-done.2
  223.9 0.0 copy-done.3
  223.9 0.0 copy-start.1
  223.9 0.0 copy-start.4
  223.9 5.4 %convolution_convert_fusion.1 = bf16[1024,3072]{1,0:T(8,128)(2,1)} fusion(bf16[512,1024]{1,0:T(8,128)(2,1)S(1)} %copy-done.3, bf16[512,3072]{1,0:T(8,128)(2,1)S(1)} %bitcast.10), kind=kOutput, calls=%fused_computation.1 | convolution fusion | flops 3224371200 | bytes 10485760 | tf_op jit(solution)/shard_map/dot_general | solution.py:26
  229.3 0.0 copy-done.1
  229.3 0.0 copy-done.4
  229.3 0.0 copy-start
  229.3 5.4 %convolution_convert_fusion = bf16[3072,1024]{1,0:T(8,128)(2,1)} fusion(bf16[512,3072]{1,0:T(8,128)(2,1)S(1)} %bitcast.9, bf16[512,1024]{1,0:T(8,128)(2,1)S(1)} %copy-done.4), kind=kOutput, calls=%fused_computation | convolution fusion | flops 3224371200 | bytes 10485760 | tf_op jit(solution)/shard_map/dot_general | solution.py:26
  234.7 0.0 copy-done
  234.7 0.7 copy.10
Async XLA Ops:
  215.3 8.6 %copy-start.2 = (bf16[4,128,3072]{2,1,0:T(8,128)(2,1)S(1)}, bf16[4,128,3072]{2,1,0:T(8,128)(2,1)}, u32[]{:S(2)}) copy-start(bf16[4,128,3072]{2,1,0:T(8,128)(2,1)} %get-tuple-element.13) | copy-start | bytes 9437188
  215.3 8.6 %copy-start.3 = (bf16[512,1024]{1,0:T(8,128)(2,1)S(1)}, bf16[512,1024]{1,0:T(8,128)(2,1)}, u32[]{:S(2)}) copy-start(bf16[512,1024]{1,0:T(8,128)(2,1)} %get-tuple-element.11) | copy-start | bytes 3145732
  223.9 5.4 %copy-start.1 = (bf16[4,128,3072]{2,1,0:T(8,128)(2,1)S(1)}, bf16[4,128,3072]{2,1,0:T(8,128)(2,1)}, u32[]{:S(2)}) copy-start(bf16[4,128,3072]{2,1,0:T(8,128)(2,1)} %get-tuple-element.14) | copy-start | bytes 9437188
  223.9 5.4 %copy-start.4 = (bf16[512,1024]{1,0:T(8,128)(2,1)S(1)}, bf16[512,1024]{1,0:T(8,128)(2,1)}, u32[]{:S(2)}) copy-start(bf16[512,1024]{1,0:T(8,128)(2,1)} %get-tuple-element.15) | copy-start | bytes 3145732
  229.3 5.4 %copy-start = (bf16[128,512]{1,0:T(8,128)(2,1)S(1)}, bf16[128,512]{1,0:T(8,128)(2,1)}, u32[]{:S(2)}) copy-start(bf16[128,512]{1,0:T(8,128)(2,1)} %get-tuple-element.20) | copy-start | bytes 393220

commit v3 on v2

--- a/solution.py
+++ b/solution.py
@@ -169,49 +169,83 @@
 
     pl.semaphore_wait(barrier, 7 + jnp.where(me != z, 1, 0))
 
-    def along_z(k):
-        return send(zbuf.at[z], zbuf.at[z], gs_sem.at[0, k], gr_sem.at[0, z], me, 2 * ((z + k) % 4) + h)
-
-    def to_owner(block):
-        return send(zbuf.at[block], gath.at[me, h], gs_sem.at[1, block], gr_sem.at[1, me], block, rep)
-
-    def to_core(owner):
-        return send(gath.at[owner, h], gath.at[owner, h], gs_sem.at[2, owner], gr_sem.at[2, owner], me, sibling)
+    total[...] = jnp.zeros_like(total)
+
+    def upward(block, kind):
+        here = zbuf.at[block, kind]
+        return send(here, here, gs_sem.at[0, kind, block], gr_sem.at[0, kind, block], me, rep + 2)
+
+    def downward(block, kind):
+        here = zbuf.at[block, kind]
+        return send(here, here, gs_sem.at[1, kind, block], gr_sem.at[0, kind, block], me, rep - 2)
+
+    def to_owner(block, kind):
+        return send(
+            zbuf.at[block, kind], gath.at[me, h, kind],
+            gs_sem.at[2, kind, block], gr_sem.at[1, kind, me], block, rep,
+        )
+
+    def to_core(owner, kind):
+        here = gath.at[owner, h, kind]
+        return send(here, here, gs_sem.at[3, kind, owner], gr_sem.at[2, kind, owner], me, sibling)
 
     def arrived(target, sem):
         pltpu.make_async_copy(target, target, sem).wait()
 
-    def pass_on(block):
+    def pass_on(block, kind):
         @pl.when(block != me)
         def _():
-            to_owner(block).start()
+            to_owner(block, kind).start()
 
         @pl.when(block == me)
         def _():
-            gath[me, h] = zbuf[block]
-            to_core(me).start()
-
-    for k in (1, 3, 2):
-        along_z(k).start()
-    pass_on(z)
-    for k in (1, 3, 2):
-        block = (z + k) % 4
-        arrived(zbuf.at[block], gr_sem.at[0, block])
-        pass_on(block)
-    for k in (1, 2, 3):
-        owner = (me + k) % 4
-        arrived(gath.at[owner, h], gr_sem.at[1, owner])
-        to_core(owner).start()
-    for k in range(4):
-        owner = (me + k) % 4
-        arrived(gath.at[owner, 1 - h], gr_sem.at[2, owner])
-    for owner in range(4):
-        for half in range(2):
-            place = (pl.ds(owner * rows, rows), pl.ds(half * feats, feats))
-            x_ref[place] = gath[owner, half, 0]
-            dy_ref[place] = gath[owner, half, 1]
-
-    total[...] = jnp.zeros_like(total)
+            gath[me, h, kind] = zbuf[block, kind]
+            to_core(me, kind).start()
+
+    def relay(block, kind, go, copy):
+        @pl.when(go)
+        def _():
+            copy(block, kind).start()
+
+    for kind in range(2):
+        relay(z, kind, z < 3, upward)
+        relay(z, kind, z > 0, downward)
+    for kind in range(2):
+        pass_on(z, kind)
+    for k in range(1, 4):
+        for kind in range(2):
+            for block, there, go, copy in (
+                (z - k, z >= k, z < 3, upward), (z + k, z + k < 4, z > 0, downward),
+            ):
+                @pl.when(there)
+                def _(block=block, kind=kind, go=go, copy=copy):
+                    arrived(zbuf.at[block, kind], gr_sem.at[0, kind, block])
+                    relay(block, kind, go, copy)
+                    pass_on(block, kind)
+
+    for kind in range(2):
+        for k in range(1, 4):
+            owner = (me + k) % 4
+            arrived(gath.at[owner, h, kind], gr_sem.at[1, kind, owner])
+            to_core(owner, kind).start()
+    for kind, target in enumerate((x_ref, dy_ref)):
+        for k in range(4):
+            owner = (me + k) % 4
+            arrived(gath.at[owner, 1 - h, kind], gr_sem.at[2, kind, owner])
+        for owner in range(4):
+            for side in range(2):
+                place = (pl.ds(owner * rows, rows), pl.ds(side * feats, feats))
+                target[place] = gath[owner, side, kind]
+
+    low, high = pl.ds(0, n // 2), pl.ds(n // 2, n - n // 2)
+
+    def hidden_copy(k):
+        part_of, owner, device = (
+            (low, me, near_x), (high, me, near_y), (high, me, near_x), (low, me, near_y),
+            (low, near_x, near_y), (high, near_y, near_x),
+        )[k]
+        block = hid.at[part_of, owner]
+        return send(block, block, hs_sem.at[k], hr_sem.at[k], device, rep)
 
     @pl.loop(0, n + 4 * LAG)
     def _(step):
@@ -277,17 +311,20 @@
             for stage in range(6):
                 remote(stage, c).wait_send()
 
-    low, high = pl.ds(0, n // 2), pl.ds(n // 2, n - n // 2)
-
-    def hidden_copy(k):
-        part_of, owner, device = (
-            (low, me, near_x), (high, me, near_y), (high, me, near_x), (low, me, near_y),
-            (low, near_x, near_y), (high, near_y, near_x),
-        )[k]
-        block = hid.at[part_of, owner]
-        return send(block, block, hs_sem.at[k], hr_sem.at[k], device, rep)
-
-    for k in range(4):
+        @pl.when(step == LAG)
+        def _():
+            scale = 1.0 / math.sqrt(HB)
+            for b in range(x_ref.shape[1] // HB):
+                columns = pl.ds(b * HB, HB)
+                xt_out[columns, :] = (dot_dims(sign_ref[...], x_ref[:, columns], 1, 1) * scale).astype(BF16)
+                dyt_out[:, columns] = (dot_dims(dy_ref[:, columns], sign_ref[...], 1, 0) * scale).astype(BF16)
+
+        @pl.when(step == n + LAG)
+        def _():
+            hidden_copy(0).start()
+            hidden_copy(3).start()
+
+    for k in (1, 2):
         hidden_copy(k).start()
 
     def half(core):
@@ -295,12 +332,6 @@
 
     fold = send(total.at[:, half(1 - h)], e1recv, es_sem.at[0], er_sem.at[0], me, sibling)
     fold.start()
-    scale = 1.0 / math.sqrt(HB)
-    for source, target in ((x_ref, xt_out), (dy_ref, dyt_out)):
-        for b in range(source.shape[1] // HB):
-            columns = pl.ds(b * HB, HB)
-            turned = jnp.dot(source[:, columns], sign_ref[...], preferred_element_type=F32)
-            target[:, columns] = (turned * scale).astype(BF16)
     fold.wait()
     for t in range(4):
         block = pl.ds(t * rows, rows)
@@ -347,13 +378,21 @@
         hidden_copy(k).wait_send()
     for k in range(1, 4):
         piece(k).wait_send()
-        along_z(k).wait_send()
-    for block in range(4):
-        @pl.when(block != me)
-        def _():
-            to_owner(block).wait_send()
-
-        to_core(block).wait_send()
+    for kind in range(2):
+        for block in range(4):
+            @pl.when((z >= block) & (z < 3))
+            def _(block=block, kind=kind):
+                upward(block, kind).wait_send()
+
+            @pl.when((z <= block) & (z > 0))
+            def _(block=block, kind=kind):
+                downward(block, kind).wait_send()
+
+            @pl.when(block != me)
+            def _(block=block, kind=kind):
+                to_owner(block, kind).wait_send()
+
+            to_core(block, kind).wait_send()
 
     @pl.loop(0, n)
     def _(c):
@@ -370,11 +409,11 @@
     signs = (hadamard(HB) * math.sqrt(HB)).astype(BF16)
     whole, anywhere = pl.BlockSpec(memory_space=pltpu.VMEM), pl.BlockSpec(memory_space=pl.ANY)
     wide = jax.ShapeDtypeStruct((4, rows, units), BF16)
-    turned = jax.ShapeDtypeStruct((count, width), BF16)
+    turned = [jax.ShapeDtypeStruct(dims, BF16) for dims in ((width, count), (count, width))]
     dma = pltpu.SemaphoreType.DMA
     hidden, d_gate, d_up, grad_tokens, x_turned, dy_turned = pl.pallas_call(
         functools.partial(fused_kernel, n),
-        out_shape=(wide, wide, wide, jax.ShapeDtypeStruct((rows, feats), BF16), turned, turned),
+        out_shape=(wide, wide, wide, jax.ShapeDtypeStruct((rows, feats), BF16), *turned),
         in_specs=[whole] * 3 + [anywhere] * 3,
         out_specs=(anywhere,) * 3 + (whole,) * 3,
         scratch_shapes=[
@@ -398,7 +437,7 @@
             pltpu.VMEM((rows, feats), BF16),
             pltpu.VMEM((rows, feats), BF16),
             dma((3, n)), dma((3, n)), dma((6, n)), dma((6, n)),
-            dma((3, 4)), dma((3, 4)), dma((6,)), dma((6,)), dma((5,)), dma((6,)),
+            dma((4, 2, 4)), dma((3, 2, 4)), dma((6,)), dma((6,)), dma((5,)), dma((6,)),
         ],
         compiler_params=pltpu.CompilerParams(
             collective_id=0, has_side_effects=True, vmem_limit_bytes=62 * 2**20
@@ -408,31 +447,52 @@
         ),
     )(tokens, grad_out, signs, w_gate, w_up, w_down)
     flat = [v.reshape(count, units) for v in (hidden, d_gate, d_up)]
-    return (*flat, grad_tokens, x_turned, dy_turned)
+    return (grad_tokens, *gradients(x_turned, dy_turned, *flat))
+
+
+def gradients_kernel(x_ref, dy_ref, hid_ref, dg_ref, du_ref, gate_ref, up_ref, down_ref):
+    gate_ref[...] = jnp.dot(x_ref[...], dg_ref[...], preferred_element_type=F32).astype(BF16)
+    up_ref[...] = jnp.dot(x_ref[...], du_ref[...], preferred_element_type=F32).astype(BF16)
+    down_ref[...] = dot_dims(hid_ref[...], dy_ref[...], 0, 0).astype(BF16)
+
+
+def gradients(x_turned, dy_turned, hidden, d_gate, d_up):
+    width, count = x_turned.shape
+    units = hidden.shape[1]
+    tile = 512
+    once = [pl.BlockSpec(dims, lambda i: (0, 0)) for dims in ((width, count), (count, width))]
+    act = pl.BlockSpec((count, tile), lambda i: (0, i))
+    grad = pl.BlockSpec((width, tile), lambda i: (0, i))
+    wide = jax.ShapeDtypeStruct((width, units), BF16)
+    return pl.pallas_call(
+        gradients_kernel,
+        grid=(units // tile,),
+        out_shape=(wide, wide, jax.ShapeDtypeStruct((units, width), BF16)),
+        in_specs=[*once, act, act, act],
+        out_specs=(grad, grad, pl.BlockSpec((tile, width), lambda i: (i, 0))),
+        compiler_params=pltpu.CompilerParams(vmem_limit_bytes=48 * 2**20),
+        cost_estimate=pl.CostEstimate(
+            flops=6 * count * width * units, bytes_accessed=12 * width * units, transcendentals=0
+        ),
+    )(x_turned, dy_turned, hidden, d_gate, d_up)
 
 
 def plain(n_rep, n_fsdp, tokens, grad_out, w_gate, w_up, w_down):
     x_block, dy_block = gather_blocks(tokens, grad_out)
     hidden, d_gate, d_up, partial = middle_plain(x_block, dy_block, w_gate, w_up, w_down)
     grad_tokens = scatter_tokens(partial, n_rep, n_fsdp)
-    return hidden, d_gate, d_up, grad_tokens, rotate_features(x_block), rotate_features(dy_block)
+    x_turned, dy_turned = rotate_features(x_block), rotate_features(dy_block)
+    return (
+        grad_tokens,
+        dot_dims(x_turned, d_gate, 0, 0).astype(BF16),
+        dot_dims(x_turned, d_up, 0, 0).astype(BF16),
+        dot_dims(hidden, dy_turned, 0, 0).astype(BF16),
+    )
 
 
 def solution(mesh):
     n_rep, n_fsdp = mesh.shape["rep"], mesh.shape["fsdp"]
-    whole = fused if (n_rep, n_fsdp) == (8, 4) else functools.partial(plain, n_rep, n_fsdp)
-
-    def body(tokens, grad_out, w_gate, w_up, w_down):
-        hidden, d_gate, d_up, grad_tokens, x_turned, dy_turned = whole(
-            tokens, grad_out, w_gate, w_up, w_down
-        )
-        return (
-            grad_tokens,
-            dot_dims(x_turned, d_gate, 0, 0).astype(BF16),
-            dot_dims(x_turned, d_up, 0, 0).astype(BF16),
-            dot_dims(hidden, dy_turned, 0, 0).astype(BF16),
-        )
-
+    body = fused if (n_rep, n_fsdp) == (8, 4) else functools.partial(plain, n_rep, n_fsdp)
     return jax.shard_map(
         body,
         mesh=mesh,

time: 235 us -> 227 us (0.966)
  matrix products: 19.3 us -> 0 us
  Pallas kernels: 214 us -> 220 us
  local copies, waits for them, and re-layouts: 0.68 us -> 4.99 us
    dot_general x3 -> x0, matrix products: 19.3 us -> none  [dot_dims(): lax.dot_general(left, right, (((left_dim,), (right_dim,)), ((), ())), pre...]
    pallas_call x0 -> x1, Pallas kernels: none -> 13.5 us  [gradients(): pl.pallas_call(gradients_kernel, grid=(units // tile,), out_shape=(wide,...]
    pallas_call x1, Pallas kernels: 214 us -> 207 us  [fused(): pl.pallas_call(functools.partial(fused_kernel, n), out_shape=(wide, wide,...]
    unnamed x11 -> x9, local copies, waits for them, and re-layouts: 0.68 us -> 4.99 us
where the time goes in v3:
time: 227 us; the launch traced here: 226 us
  Pallas kernels  220 us (97%)
  local copies, waits for them, and re-layouts  4.99 us (2%)
    pallas_call x1, Pallas kernels, fused(): pl.pallas_call(functools.partial(fused_kernel, n), out_shape=(wide, wide,...  207 us
    pallas_call x1, Pallas kernels, gradients(): pl.pallas_call(gradients_kernel, grid=(units // tile,), out_shape=(wide,...  13.5 us
    unnamed x9, local copies, waits for them, and re-layouts  4.99 us

profile of v3, /device:TPU:2, one launch (start us, length us, event | category | flops | bytes accessed | tf_op | source)
XLA Modules:
  0.0 226.5 jit_solution(4284694392614380941)
XLA Ops:
  0.6 0.7 fusion.5.sign_ref
  1.3 206.6 %shard_map.84 = (bf16[4,128,3072]{2,1,0:T(8,128)(2,1)}, bf16[4,128,3072]{2,1,0:T(8,128)(2,1)}, bf16[4,128,3072]{2,1,0:T(8,128)(2,1)}, bf16[128,512]{1,0:T(8,128)...) custom-call(bf16[128,512]{1,0:T(8,128)(2,1)} %tok_ref.1, bf16[128,512]{1,0:T(8,128)(2,1)} %go_ref.1, ...), custom_call_target="tpu_custom_call" | custom-call | flops 16106127360 | bytes 37748736 | tf_op jit(solution)/shard_map/pallas_call | solution.py:414
  208.0 0.0 copy-start
  208.0 1.9 copy-done
  209.9 0.0 copy-start.1
  209.9 1.2 copy-done.1
  211.1 0.0 copy-start.2
  211.1 1.2 copy-done.2
  212.3 0.0 copy-start.3
  212.3 13.5 %shard_map.85 = (bf16[1024,3072]{1,0:T(8,128)(2,1)}, bf16[1024,3072]{1,0:T(8,128)(2,1)}, bf16[3072,1024]{1,0:T(8,128)(2,1)}) custom-call(bf16[1024,512]{1,0:T(8,128)(2,1)S(1)} %copy-done.1, bf16[512,1024]{1,0:T(8,128)(2,1)S(1)} %copy-done.2, bf16[512,3072]{1,0:T(8,128)(2,1)S(1)} %bitcast.3, bf16[512,3072]{1,0:T(8,128)(2,1)} %bitcast.4, bf16[512,3072]{1,0:T(8,128)(2,1)} %bitcast.5), custom_call_target="tpu_custom_call" | custom-call | flops 9663676416 | bytes 37748736 | tf_op jit(solution)/shard_map/pallas_call | solution.py:467
  225.8 0.0 copy-done.3
  225.8 0.7 copy.10
Async XLA Ops:
  208.0 1.9 copy-start
  209.9 1.2 copy-start.1
  211.1 1.2 copy-start.2
  212.3 13.5 %copy-start.3 = (bf16[128,512]{1,0:T(8,128)(2,1)S(1)}, bf16[128,512]{1,0:T(8,128)(2,1)}, u32[]{:S(2)}) copy-start(bf16[128,512]{1,0:T(8,128)(2,1)} %get-tuple-element.26) | copy-start | bytes 393220

commit v4 on v3

--- a/solution.py
+++ b/solution.py
@@ -81,7 +81,8 @@
 
 
 MESH = pl.DeviceIdType.MESH
-LAG = 2
+LAG = 3
+EARLY = 4
 
 
 def fused_kernel(
@@ -109,13 +110,14 @@
             device_id={"rep": to, "fsdp": fsdp}, device_id_type=MESH,
         )
 
-    def weights(c):
+    def weight(k, c):
         columns = span(c, chunk)
-        return (
-            pltpu.make_async_copy(wg_hbm.at[:, columns], w_pair.at[c, :, pl.ds(0, chunk)], w_sem.at[0, c]),
-            pltpu.make_async_copy(wu_hbm.at[:, columns], w_pair.at[c, :, pl.ds(chunk, chunk)], w_sem.at[1, c]),
-            pltpu.make_async_copy(wd_hbm.at[columns, :], w_low.at[c], w_sem.at[2, c]),
-        )
+        source, target = (
+            (wg_hbm.at[:, columns], w_pair.at[c, :, pl.ds(0, chunk)]),
+            (wu_hbm.at[:, columns], w_pair.at[c, :, pl.ds(chunk, chunk)]),
+            (wd_hbm.at[columns, :], w_low.at[c]),
+        )[k]
+        return pltpu.make_async_copy(source, target, w_sem.at[k, c])
 
     def results(c):
         return [
@@ -134,19 +136,21 @@
     def remote(stage, c):
         first, second = partners(c)
         source, target, device = (
-            (send1.at[c, 0], recv1.at[c, 0], first),
-            (send1.at[c, 1], recv1.at[c, 1], first),
+            (send1.at[c, 0, pl.ds(0, 2)], recv1.at[c, 0, pl.ds(0, 2)], first),
+            (send1.at[c, 1, pl.ds(0, 2)], recv1.at[c, 1, pl.ds(0, 2)], first),
             (send2.at[c], recv2.at[c], second),
             (acts.at[c, me], acts.at[c, me], first),
             (acts.at[c, me], acts.at[c, me], second),
             (acts.at[c, first], acts.at[c, first], second),
+            (send1.at[c, 0, 2], recv1.at[c, 0, 2], first),
+            (send1.at[c, 1, 2], recv1.at[c, 1, 2], first),
         )[stage]
         return send(source, target, ssem.at[stage, c], rsem.at[stage, c], device, rep)
 
     @pl.loop(0, n)
     def _(c):
-        for copy in weights(c):
-            copy.start()
+        for k in range(3):
+            weight(k, c).start()
 
     zbuf[z, 0] = tok_ref[...]
     zbuf[z, 1] = go_ref[...]
@@ -207,28 +211,28 @@
         def _():
             copy(block, kind).start()
 
-    for kind in range(2):
+    def own(kind):
         relay(z, kind, z < 3, upward)
         relay(z, kind, z > 0, downward)
-    for kind in range(2):
         pass_on(z, kind)
-    for k in range(1, 4):
-        for kind in range(2):
-            for block, there, go, copy in (
-                (z - k, z >= k, z < 3, upward), (z + k, z + k < 4, z > 0, downward),
-            ):
-                @pl.when(there)
-                def _(block=block, kind=kind, go=go, copy=copy):
-                    arrived(zbuf.at[block, kind], gr_sem.at[0, kind, block])
-                    relay(block, kind, go, copy)
-                    pass_on(block, kind)
-
-    for kind in range(2):
+
+    def from_afar(k, kind):
+        for block, there, go, copy in (
+            (z - k, z >= k, z < 3, upward), (z + k, z + k < 4, z > 0, downward),
+        ):
+            @pl.when(there)
+            def _(block=block, go=go, copy=copy):
+                arrived(zbuf.at[block, kind], gr_sem.at[0, kind, block])
+                relay(block, kind, go, copy)
+                pass_on(block, kind)
+
+    def hand_over(kind):
         for k in range(1, 4):
             owner = (me + k) % 4
             arrived(gath.at[owner, h, kind], gr_sem.at[1, kind, owner])
             to_core(owner, kind).start()
-    for kind, target in enumerate((x_ref, dy_ref)):
+
+    def assemble(kind, target):
         for k in range(4):
             owner = (me + k) % 4
             arrived(gath.at[owner, 1 - h, kind], gr_sem.at[2, kind, owner])
@@ -237,6 +241,43 @@
                 place = (pl.ds(owner * rows, rows), pl.ds(side * feats, feats))
                 target[place] = gath[owner, side, kind]
 
+    def start_pair(c):
+        slot = lax.rem(c, slots)
+        first, _ = partners(c)
+        for k in range(2):
+            weight(k, c).wait()
+        pair = jnp.dot(x_ref[...], w_pair[c], preferred_element_type=F32)
+        part[slot, :, 0] = pair[:, :chunk].reshape(4, -1, chunk)
+        part[slot, :, 1] = pair[:, chunk:].reshape(4, -1, chunk)
+        for stage, block in enumerate((far, first)):
+            for k in range(2):
+                send1[c, stage, k] = part[slot, block, k].astype(BF16)
+            remote(stage, c).start()
+
+    def start_low(c):
+        slot = lax.rem(c, slots)
+        first, _ = partners(c)
+        weight(2, c).wait()
+        part[slot, :, 2] = dot_dims(dy_ref[...], w_low[c], 1, 1).reshape(4, -1, chunk)
+        for stage, block in enumerate((far, first)):
+            send1[c, stage, 2] = part[slot, block, 2].astype(BF16)
+            remote(6 + stage, c).start()
+
+    own(0)
+    from_afar(1, 0)
+    own(1)
+    from_afar(2, 0)
+    from_afar(1, 1)
+    from_afar(3, 0)
+    from_afar(2, 1)
+    hand_over(0)
+    assemble(0, x_ref)
+    pl.loop(0, EARLY // 2)(start_pair)
+    from_afar(3, 1)
+    hand_over(1)
+    pl.loop(EARLY // 2, EARLY)(start_pair)
+    assemble(1, dy_ref)
+
     low, high = pl.ds(0, n // 2), pl.ds(n // 2, n - n // 2)
 
     def hidden_copy(k):
@@ -251,19 +292,11 @@
     def _(step):
         @pl.when(step < n)
         def _():
-            c = step
-            slot = lax.rem(c, slots)
-            for copy in weights(c):
-                copy.wait()
-            pair = jnp.dot(x_ref[...], w_pair[c], preferred_element_type=F32)
-            part[slot, :, 0] = pair[:, :chunk].reshape(4, -1, chunk)
-            part[slot, :, 1] = pair[:, chunk:].reshape(4, -1, chunk)
-            part[slot, :, 2] = dot_dims(dy_ref[...], w_low[c], 1, 1).reshape(4, -1, chunk)
-            first, _ = partners(c)
-            send1[c, 0] = part[slot, far].astype(BF16)
-            remote(0, c).start()
-            send1[c, 1] = part[slot, first].astype(BF16)
-            remote(1, c).start()
+            @pl.when(step >= EARLY)
+            def _():
+                start_pair(step)
+
+            start_low(step)
 
         @pl.when((step >= LAG) & (step < n + LAG))
         def _():
@@ -271,6 +304,7 @@
             slot = lax.rem(c, slots)
             _, second = partners(c)
             remote(0, c).wait_recv()
+            remote(6, c).wait_recv()
             send2[c] = (part[slot, second] + recv1[c, 0].astype(F32)).astype(BF16)
             remote(2, c).start()
 
@@ -279,6 +313,7 @@
             c = step - 2 * LAG
             slot = lax.rem(c, slots)
             remote(1, c).wait_recv()
+            remote(7, c).wait_recv()
             remote(2, c).wait_recv()
             sums = [
                 part[slot, me, k] + recv1[c, 1, k].astype(F32) + recv2[c, k].astype(F32)
@@ -308,7 +343,7 @@
                 [acts[c, :, 0].reshape(-1, chunk), acts[c, :, 1].reshape(-1, chunk)], axis=1
             )
             total[...] += dot_dims(pair, w_pair[c], 1, 1)
-            for stage in range(6):
+            for stage in range(8):
                 remote(stage, c).wait_send()
 
         @pl.when(step == LAG)
@@ -436,7 +471,7 @@
             pltpu.VMEM((4, rows, feats), BF16),
             pltpu.VMEM((rows, feats), BF16),
             pltpu.VMEM((rows, feats), BF16),
-            dma((3, n)), dma((3, n)), dma((6, n)), dma((6, n)),
+            dma((3, n)), dma((3, n)), dma((8, n)), dma((8, n)),
             dma((4, 2, 4)), dma((3, 2, 4)), dma((6,)), dma((6,)), dma((5,)), dma((6,)),
         ],
         compiler_params=pltpu.CompilerParams(
@@ -459,7 +494,7 @@
 def gradients(x_turned, dy_turned, hidden, d_gate, d_up):
     width, count = x_turned.shape
     units = hidden.shape[1]
-    tile = 512
+    tile = 256
     once = [pl.BlockSpec(dims, lambda i: (0, 0)) for dims in ((width, count), (count, width))]
     act = pl.BlockSpec((count, tile), lambda i: (0, i))
     grad = pl.BlockSpec((width, tile), lambda i: (0, i))
@@ -470,7 +505,7 @@
         out_shape=(wide, wide, jax.ShapeDtypeStruct((units, width), BF16)),
         in_specs=[*once, act, act, act],
         out_specs=(grad, grad, pl.BlockSpec((tile, width), lambda i: (i, 0))),
-        compiler_params=pltpu.CompilerParams(vmem_limit_bytes=48 * 2**20),
+        compiler_params=pltpu.CompilerParams(vmem_limit_bytes=60 * 2**20),
         cost_estimate=pl.CostEstimate(
             flops=6 * count * width * units, bytes_accessed=12 * width * units, transcendentals=0
         ),

time: 227 us -> 221 us (0.974)
  local copies, waits for them, and re-layouts: 4.99 us -> 0.66 us
    pallas_call x1, Pallas kernels: 207 us -> 202 us  [fused(): pl.pallas_call(functools.partial(fused_kernel, n), out_shape=(wide, wide,...]
    unnamed x9 -> x3, local copies, waits for them, and re-layouts: 4.99 us -> 0.66 us
    pallas_call x1, Pallas kernels: 13.5 us -> 17 us  [gradients(): pl.pallas_call(gradients_kernel, grid=(units // tile,), out_shape=(wide,...]
where the time goes in v4:
time: 221 us
  Pallas kernels  219 us (99%)
    pallas_call x1, Pallas kernels, fused(): pl.pallas_call(functools.partial(fused_kernel, n), out_shape=(wide, wide,...  202 us
    pallas_call x1, Pallas kernels, gradients(): pl.pallas_call(gradients_kernel, grid=(units // tile,), out_shape=(wide,...  17 us

profile of v4, /device:TPU:2, one launch (start us, length us, event | category | flops | bytes accessed | tf_op | source)
XLA Modules:
  0.0 221.0 jit_solution(785633718942399874)
XLA Ops:
  0.6 0.7 fusion.5.sign_ref
  1.3 202.0 %shard_map.84 = (bf16[4,128,3072]{2,1,0:T(8,128)(2,1)}, bf16[4,128,3072]{2,1,0:T(8,128)(2,1)}, bf16[4,128,3072]{2,1,0:T(8,128)(2,1)}, bf16[128,512]{1,0:T(8,128)...) custom-call(bf16[128,512]{1,0:T(8,128)(2,1)} %tok_ref.1, bf16[128,512]{1,0:T(8,128)(2,1)} %go_ref.1, ...), custom_call_target="tpu_custom_call" | custom-call | flops 16106127360 | bytes 37748736 | tf_op jit(solution)/shard_map/pallas_call | solution.py:449
  203.3 0.0 copy-start
  203.3 17.0 %shard_map.85 = (bf16[1024,3072]{1,0:T(8,128)(2,1)}, bf16[1024,3072]{1,0:T(8,128)(2,1)}, bf16[3072,1024]{1,0:T(8,128)(2,1)}) custom-call(bf16[1024,512]{1,0:T(8,128)(2,1)} %get-tuple-element.14.x_ref, bf16[512,1024]{1,0:T(8,128)(2,1)} %get-tuple-element.15.dy_ref, bf16[512,3072]{1,0:T(8,128)(2,1)} %bitcast.3, bf16[512,3072]{1,0:T(8,128)(2,1)} %bitcast.4, ...), custom_call_target="tpu_custom_call" | custom-call | flops 9663676416 | bytes 37748736 | tf_op jit(solution)/shard_map/pallas_call | solution.py:502
  220.3 0.0 copy-done
  220.3 0.7 copy.10
Async XLA Ops:
  203.3 17.0 %copy-start = (bf16[128,512]{1,0:T(8,128)(2,1)S(1)}, bf16[128,512]{1,0:T(8,128)(2,1)}, u32[]{:S(2)}) copy-start(bf16[128,512]{1,0:T(8,128)(2,1)} %get-tuple-element.26) | copy-start | bytes 393220

commit v5 on v4

--- a/solution.py
+++ b/solution.py
@@ -494,7 +494,7 @@
 def gradients(x_turned, dy_turned, hidden, d_gate, d_up):
     width, count = x_turned.shape
     units = hidden.shape[1]
-    tile = 256
+    tile = 512
     once = [pl.BlockSpec(dims, lambda i: (0, 0)) for dims in ((width, count), (count, width))]
     act = pl.BlockSpec((count, tile), lambda i: (0, i))
     grad = pl.BlockSpec((width, tile), lambda i: (0, i))

time: 221 us -> 219 us (level)
  Pallas kernels: 219 us -> 216 us
    pallas_call x1, Pallas kernels: 17 us -> 14.5 us  [gradients(): pl.pallas_call(gradients_kernel, grid=(units // tile,), out_shape=(wide,...]
where the time goes in v5:
time: 219 us; the launch traced here: 218 us
  Pallas kernels  216 us (99%)
    pallas_call x1, Pallas kernels, fused(): pl.pallas_call(functools.partial(fused_kernel, n), out_shape=(wide, wide,...  202 us
    pallas_call x1, Pallas kernels, gradients(): pl.pallas_call(gradients_kernel, grid=(units // tile,), out_shape=(wide,...  14.5 us

profile of v5, /device:TPU:2, one launch (start us, length us, event | category | flops | bytes accessed | tf_op | source)
XLA Modules:
  0.0 218.5 jit_solution(2656800855455384948)
XLA Ops:
  0.6 0.7 fusion.5.sign_ref
  1.3 202.0 %shard_map.84 = (bf16[4,128,3072]{2,1,0:T(8,128)(2,1)}, bf16[4,128,3072]{2,1,0:T(8,128)(2,1)}, bf16[4,128,3072]{2,1,0:T(8,128)(2,1)}, bf16[128,512]{1,0:T(8,128)...) custom-call(bf16[128,512]{1,0:T(8,128)(2,1)} %tok_ref.1, bf16[128,512]{1,0:T(8,128)(2,1)} %go_ref.1, ...), custom_call_target="tpu_custom_call" | custom-call | flops 16106127360 | bytes 37748736 | tf_op jit(solution)/shard_map/pallas_call | solution.py:449
  203.3 0.0 copy-start
  203.3 14.5 %shard_map.85 = (bf16[1024,3072]{1,0:T(8,128)(2,1)}, bf16[1024,3072]{1,0:T(8,128)(2,1)}, bf16[3072,1024]{1,0:T(8,128)(2,1)}) custom-call(bf16[1024,512]{1,0:T(8,128)(2,1)} %get-tuple-element.14.x_ref, bf16[512,1024]{1,0:T(8,128)(2,1)} %get-tuple-element.15.dy_ref, bf16[512,3072]{1,0:T(8,128)(2,1)} %bitcast.3, bf16[512,3072]{1,0:T(8,128)(2,1)} %bitcast.4, ...), custom_call_target="tpu_custom_call" | custom-call | flops 9663676416 | bytes 37748736 | tf_op jit(solution)/shard_map/pallas_call | solution.py:502
  217.8 0.0 copy-done
  217.8 0.7 copy.10
Async XLA Ops:
  203.3 14.5 %copy-start = (bf16[128,512]{1,0:T(8,128)(2,1)S(1)}, bf16[128,512]{1,0:T(8,128)(2,1)}, u32[]{:S(2)}) copy-start(bf16[128,512]{1,0:T(8,128)(2,1)} %get-tuple-element.26) | copy-start | bytes 393220
